TPU v7x, 32 devices: a whole 2x2x4 slice. The times are simulated.
32 devices in a mesh: rows: 8 (over z, y), snaps: 4 (over x, core).
Axes of the slice: x: 2, y: 2, z: 4, core: 2. Of those that a mesh axis runs over, the one named last changes fastest.
Arguments:
- stress: float32 [131072, 1024], P('rows', 'snaps'), may hold values from -80 to 80
- sketch: float32 [64, 1024], P(None, 'snaps'), may hold values from -0.1875 to 0.1875
Outputs:
- basis: float32 [64, 131072], P(None, ('rows', 'snaps'))
- coeffs: float32 [64, 1024], P(None, 'snaps')
- spectrum: float32 [64, 64], replicated
All inputs are finite; a program needn't handle non-finite values.
Results may differ from a plain program's by a relative error of at most 0.0015.
Values sent between devices are 32-bit elements; how exact they have to be, the bound alone decides.
A program may use at most 128 MiB of HBM per device.

v0:
```python
import math
import jax
import jax.numpy as jnp
from jax import lax
from jax.sharding import PartitionSpec as P


def product(left_m, right_m, left_dim, right_dim):
    return lax.dot_general(
        left_m,
        right_m,
        (((left_dim,), (right_dim,)), ((), ())),
        precision=lax.Precision.HIGHEST,
        preferred_element_type=jnp.float32,
    )


def inverse_factor(gram_total):
    lower = jnp.linalg.cholesky(gram_total)
    ident = jnp.eye(gram_total.shape[0], dtype=gram_total.dtype)
    return lax.linalg.triangular_solve(lower, ident, left_side=True, lower=True)


def section_whole(panel, stress):
    factor = inverse_factor(lax.psum(product(panel, panel, 1, 1), "rows"))
    basis = product(factor, panel, 1, 0)
    coeffs = lax.psum(product(basis, stress, 1, 0), "rows")
    return (basis, coeffs)


def on_device(stress, sketch):
    rows_dev = stress.shape[0]
    groups = lax.axis_size("snaps")
    share = rows_dev // groups
    operand = sketch
    basis = None
    for turn in range(2):
        partial_value = product(operand, stress, 1, 1)
        panel = lax.psum(partial_value, "snaps")
        basis, operand = section_whole(panel, stress)
    basis = lax.dynamic_slice_in_dim(basis, lax.axis_index("snaps") * share, share, 1)
    scale = math.sqrt(float(rows_dev * lax.axis_size("rows")))
    batch_total = operand.shape[1] * groups
    spectrum = lax.psum(product(operand, operand, 1, 1), "snaps") / batch_total
    return (basis * scale, operand, spectrum)


def solution(mesh):
    placed = (P("rows", "snaps"), P(None, "snaps"))
    return jax.shard_map(
        on_device,
        mesh=mesh,
        in_specs=placed,
        out_specs=(P(None, ("rows", "snaps")), P(None, "snaps"), P()),
        check_vma=False,
    )
```

profile of v0, /device:TPU:0, one launch (start us, length us, event | category | flops | bytes accessed | tf_op | source)
XLA Modules:
  0.0 522.6 jit_solution(17021512674975102727)
XLA Ops:
  7.2 0.0 copy-start
  7.2 0.0 all-reduce.5.cloned.1.call-start
  7.2 0.8 copy-done
  8.0 20.6 %fusion.12 = f32[64,16384]{1,0:T(8,128)} fusion(f32[64,256]{1,0:T(8,128)S(1)} %copy-done, f32[16384,256]{1,0:T(8,128)} %param.5), kind=kOutput, calls=%fused_computation.23 | convolution fusion | flops 3221225472 | bytes 21037056 | tf_op jit(solution)/shard_map/dot_general | solution.py:9
  28.6 0.0 all-reduce.5.cloned.1.call-update
  28.7 0.0 all-reduce.7.cloned.1.call-start
  28.7 88.3 %all-reduce.5.cloned.1.call-done = f32[64,16384]{1,0:T(8,128)} async-done(((f32[64,16384]{1,0:T(8,128)}), f32[64,16384]{1,0:T(8,128)}) %all-reduce.5.cloned.1.call-update) | async-done | bytes 4194320 | tf_op jit(solution)/shard_map/psum | solution.py:39
  117.0 6.9 %fusion.13 = f32[64,64]{0,1:T(8,128)S(1)} fusion(f32[64,16384]{1,0:T(8,128)} %all-reduce.5.cloned.1.call-done), kind=kOutput, calls=%fused_computation.24 | convolution fusion | flops 805306368 | bytes 4210688 | tf_op jit(solution)/shard_map/dot_general | solution.py:9
  124.0 37.2 %psum.50 = f32[64,64]{0,1:T(8,128)S(1)} all-reduce(f32[64,64]{0,1:T(8,128)S(1)} %fusion.13), channel_id=1, replica_groups=mesh['rows'=8,'snaps'=4] {'rows'}, use_global_device_ids=true, to_apply=%region_1.0 | all-reduce | flops 4096 | bytes 32768 | tf_op jit(solution)/shard_map/psum | solution.py:25
  161.1 0.1 copy.6
  161.2 5.8 %cholesky.44 = f32[64,64]{1,0:T(8,128)S(1)} custom-call(f32[64,64]{1,0:T(8,128)S(1)} %fusion.9), custom_call_target="Cholesky" | custom-call | tf_op jit(solution)/shard_map/jit(cholesky)/cholesky | solution.py:19
  167.1 0.6 compare_reduce_fusion.1
  167.7 0.7 fusion.4
  168.4 4.9 custom-call.6
  173.3 0.3 fusion.2
  173.5 5.5 %fusion.14 = f32[64,16384]{1,0:T(8,128)S(1)} fusion(f32[64,64]{1,0:T(8,128)S(1)} %fusion.2, f32[64,16384]{1,0:T(8,128)} %all-reduce.5.cloned.1.call-done), kind=kOutput, calls=%fused_computation.25 | convolution fusion | flops 805306368 | bytes 8404992 | tf_op jit(solution)/shard_map/dot_general | solution.py:9
  179.0 11.6 %fusion.15 = f32[64,256]{1,0:T(8,128)} fusion(f32[64,16384]{1,0:T(8,128)S(1)} %fusion.14, f32[16384,256]{1,0:T(8,128)} %param.5), kind=kOutput, calls=%fused_computation.26 | convolution fusion | flops 3221225472 | bytes 21037056 | tf_op jit(solution)/shard_map/dot_general | solution.py:9
  190.6 0.0 all-reduce.7.cloned.1.call-update
  190.6 0.3 all-reduce.9.cloned.1.call-start
  190.9 64.8 %all-reduce.7.cloned.1.call-done = f32[64,256]{1,0:T(8,128)} async-done(((f32[64,256]{1,0:T(8,128)}), f32[64,256]{1,0:T(8,128)}) %all-reduce.7.cloned.1.call-update) | async-done | bytes 65552 | tf_op jit(solution)/shard_map/psum | solution.py:27
  255.7 20.6 %fusion.16 = f32[64,16384]{1,0:T(8,128)} fusion(f32[64,256]{1,0:T(8,128)} %all-reduce.7.cloned.1.call-done, f32[16384,256]{1,0:T(8,128)} %param.5), kind=kOutput, calls=%fused_computation.27 | convolution fusion | flops 3221225472 | bytes 21037056 | tf_op jit(solution)/shard_map/dot_general | solution.py:9
  276.3 0.0 all-reduce.9.cloned.1.call-update
  276.4 0.0 all-reduce.11.cloned.1.call-start
  276.4 85.5 %all-reduce.9.cloned.1.call-done = f32[64,16384]{1,0:T(8,128)} async-done(((f32[64,16384]{1,0:T(8,128)}), f32[64,16384]{1,0:T(8,128)}) %all-reduce.9.cloned.1.call-update) | async-done | bytes 4194320 | tf_op jit(solution)/shard_map/psum | solution.py:39
  361.9 6.9 %fusion.17 = f32[64,64]{0,1:T(8,128)S(1)} fusion(f32[64,16384]{1,0:T(8,128)} %all-reduce.9.cloned.1.call-done), kind=kOutput, calls=%fused_computation.28 | convolution fusion | flops 805306368 | bytes 4210688 | tf_op jit(solution)/shard_map/dot_general | solution.py:9
  368.9 37.1 %psum.53 = f32[64,64]{0,1:T(8,128)S(1)} all-reduce(f32[64,64]{0,1:T(8,128)S(1)} %fusion.17), channel_id=1, replica_groups=mesh['rows'=8,'snaps'=4] {'rows'}, use_global_device_ids=true, to_apply=%region_6.9 | all-reduce | flops 4096 | bytes 32768 | tf_op jit(solution)/shard_map/psum | solution.py:25
  406.0 0.1 copy.8
  406.1 5.8 %cholesky.55 = f32[64,64]{1,0:T(8,128)S(1)} custom-call(f32[64,64]{1,0:T(8,128)S(1)} %fusion.7), custom_call_target="Cholesky" | custom-call | tf_op jit(solution)/shard_map/jit(cholesky)/cholesky | solution.py:19
  412.0 0.6 compare_reduce_fusion
  412.7 0.7 fusion.5
  413.3 4.9 custom-call.7
  418.2 0.3 fusion
  418.5 5.5 %fusion.18 = f32[64,16384]{1,0:T(8,128)S(1)} fusion(f32[64,64]{1,0:T(8,128)S(1)} %fusion, f32[64,16384]{1,0:T(8,128)} %all-reduce.9.cloned.1.call-done), kind=kOutput, calls=%fused_computation.29 | convolution fusion | flops 805306368 | bytes 8404992 | tf_op jit(solution)/shard_map/dot_general | solution.py:9
  423.9 0.0 copy-start.1
  423.9 1.9 copy-done.1
  425.9 11.6 %fusion.19 = f32[64,256]{1,0:T(8,128)} fusion(f32[64,16384]{1,0:T(8,128)S(1)} %fusion.18, f32[16384,256]{1,0:T(8,128)} %param.5), kind=kOutput, calls=%fused_computation.30 | convolution fusion | flops 3221225472 | bytes 21037056 | tf_op jit(solution)/shard_map/dot_general | solution.py:9
  437.4 0.0 all-reduce.11.cloned.1.call-update
  437.5 2.3 dynamic-slice_multiply_fusion
  439.8 62.8 %all-reduce.11.cloned.1.call-done = f32[64,256]{1,0:T(8,128)} async-done(((f32[64,256]{1,0:T(8,128)}), f32[64,256]{1,0:T(8,128)}) %all-reduce.11.cloned.1.call-update) | async-done | bytes 65552 | tf_op jit(solution)/shard_map/psum | solution.py:27
  502.5 1.1 fusion.20
  503.7 10.3 %psum.55 = f32[64,64]{1,0:T(8,128)S(1)} all-reduce(f32[64,64]{1,0:T(8,128)S(1)} %fusion.20), channel_id=1, replica_groups=mesh['rows'=8,'snaps'=4] {'snaps'}, use_global_device_ids=true, to_apply=%region_8.11 | all-reduce | flops 4096 | bytes 32768 | tf_op jit(solution)/shard_map/psum | solution.py:44
  513.9 0.6 broadcast_multiply_fusion
  514.6 1.5 copy.15
  (4 shorter events, 0.1 us)
Async XLA Ops:
  7.2 0.8 copy-start
  7.2 109.8 %all-reduce.5.cloned.1.call-start = ((), (), s32[]{:S(2)}) async-start(), calls=%async_computation | async-start | bytes 8388608 | tf_op jit(solution)/shard_map/psum | solution.py:39
  28.7 227.1 %all-reduce.7.cloned.1.call-start = ((), (), s32[]{:S(2)}) async-start(), calls=%async_computation.1 | async-start | bytes 131072 | tf_op jit(solution)/shard_map/psum | solution.py:27
  190.6 171.3 %all-reduce.9.cloned.1.call-start = ((), (), s32[]{:S(2)}) async-start(), calls=%async_computation.2 | async-start | bytes 8388608 | tf_op jit(solution)/shard_map/psum | solution.py:39
  276.4 226.2 %all-reduce.11.cloned.1.call-start = ((), (), s32[]{:S(2)}) async-start(), calls=%async_computation.3 | async-start | bytes 131072 | tf_op jit(solution)/shard_map/psum | solution.py:27
  423.9 1.9 copy-start.1
Sparse Core Ops, SparseCore 0:
  28.8 88.1 all-reduce.4
  190.8 64.9 all-reduce.6
  276.5 85.4 all-reduce.8
  437.6 64.9 all-reduce.10
where the time goes:
time: 523 us
  waiting for transfers between devices  301 us (58%)
  matrix products  90.8 us (17%)
  blocking collectives  84.6 us (16%)
  other arithmetic  27.1 us (5%)
  between operations  13.9 us (3%)
    psum x2, waiting for transfers between devices, on_device(): panel = lax.psum(partial_value, 'snaps')  174 us
    psum x2, waiting for transfers between devices, section_whole(): coeffs = lax.psum(product(basis, stress, 1, 0), 'rows')  128 us
    dot_general x9, matrix products, product(): lax.dot_general(left_m, right_m, (((left_dim,), (right_dim,)), ((), ())),...  90.3 us
    psum x2, blocking collectives, section_whole(): factor = inverse_factor(lax.psum(product(panel, panel, 1, 1), 'rows'))  74.3 us
    another operation x6, other arithmetic, inverse_factor(): lower = jnp.linalg.cholesky(gram_total)  13 us
    another operation x4, other arithmetic, inverse_factor(): return lax.linalg.triangular_solve(lower, ident, left_side=True, lower=True)  11.1 us
  transfers between devices with their start and end apart: 4, of which 4 were waited for; matrix products, arithmetic and copies ran while one was open for 0% of the time, Pallas kernels for 0%

commit v1 on v0

--- a/solution.py
+++ b/solution.py
@@ -36,7 +36,9 @@
     basis = None
     for turn in range(2):
         partial_value = product(operand, stress, 1, 1)
-        panel = lax.psum(partial_value, "snaps")
+        panel = partial_value
+        for hop in (1, 2):
+            panel = panel + lax.ppermute(panel, "snaps", [(dev, dev ^ hop) for dev in range(4)])
         basis, operand = section_whole(panel, stress)
     basis = lax.dynamic_slice_in_dim(basis, lax.axis_index("snaps") * share, share, 1)
     scale = math.sqrt(float(rows_dev * lax.axis_size("rows")))

time: 523 us -> 551 us (1.054)
  waiting for transfers between devices: 301 us -> 325 us
  matrix products: 90.8 us -> 78.5 us
  other arithmetic: 27.1 us -> 34.5 us
    ppermute x0 -> x4, waiting for transfers between devices: none -> 196 us  [on_device(): lax.ppermute(panel, 'snaps', [(dev, dev ^ hop) for dev in range(4)])]
    psum x2 -> x0, waiting for transfers between devices: 174 us -> none  [on_device(): panel = lax.psum(partial_value, 'snaps')]
    dot_general x9, matrix products: 90.3 us -> 78 us  [product(): lax.dot_general(left_m, right_m, (((left_dim,), (right_dim,)), ((), ())),...]
    add x0 -> x4, other arithmetic: none -> 7.39 us  [on_device(): panel + lax.ppermute(panel, 'snaps', [(dev, dev ^ hop) for dev in range(4)])]
  transfers between devices with their start and end apart: 4 -> 6, of which waited for: 4 -> 6; matrix products, arithmetic and copies ran while one was open for 0% -> 0% of each run, Pallas kernels for 0% -> 0%
where the time goes in v1:
time: 551 us; the launch traced here: 550 us
  waiting for transfers between devices  325 us (59%)
  blocking collectives  84.1 us (15%)
  matrix products  78.5 us (14%)
  other arithmetic  34.5 us (6%)
  between operations  14.2 us (3%)
  local copies, waits for them, and re-layouts  8.18 us (1%)
    ppermute x4, waiting for transfers between devices, on_device(): lax.ppermute(panel, 'snaps', [(dev, dev ^ hop) for dev in range(4)])  196 us
    psum x2, waiting for transfers between devices, section_whole(): coeffs = lax.psum(product(basis, stress, 1, 0), 'rows')  129 us
    dot_general x9, matrix products, product(): lax.dot_general(left_m, right_m, (((left_dim,), (right_dim,)), ((), ())),...  78 us
    psum x2, blocking collectives, section_whole(): factor = inverse_factor(lax.psum(product(panel, panel, 1, 1), 'rows'))  73.8 us
    another operation x6, other arithmetic, inverse_factor(): lower = jnp.linalg.cholesky(gram_total)  13 us
    another operation x4, other arithmetic, inverse_factor(): return lax.linalg.triangular_solve(lower, ident, left_side=True, lower=True)  11.1 us
  transfers between devices with their start and end apart: 6, of which 6 were waited for; matrix products, arithmetic and copies ran while one was open for 0% of the time, Pallas kernels for 0%

profile of v1, /device:TPU:0, one launch (start us, length us, event | category | flops | bytes accessed | tf_op | source)
XLA Modules:
  0.0 550.2 jit_solution(3900286912524273128)
XLA Ops:
  7.2 0.0 copy-start
  7.2 0.0 all-reduce.3.cloned.1.call-start
  7.2 0.8 copy-done
  8.0 18.0 %fusion.12 = f32[64,16384]{1,0:T(8,128)S(1)} fusion(f32[64,256]{1,0:T(8,128)S(1)} %copy-done, f32[16384,256]{1,0:T(8,128)} %param.5), kind=kOutput, calls=%fused_computation.23 | convolution fusion | flops 3221225472 | bytes 21037056 | tf_op jit(solution)/shard_map/dot_general | solution.py:9
  26.0 0.5 collective-permute-start
  26.5 6.8 %collective-permute-done = f32[64,16384]{1,0:T(8,128)S(1)} collective-permute-done((f32[64,16384]{1,0:T(8,128)S(1)}, f32[64,16384]{1,0:T(8,128)S(1)}, u32[]{:S(2)}, u32[]{:S(2)}) %collective-permute-start) | collective-permute-done | bytes 4194336 | tf_op jit(solution)/shard_map/ppermute | solution.py:41
  33.3 0.5 add.33
  33.8 2.9 collective-permute-start.1
  36.7 90.9 %collective-permute-done.1 = f32[64,16384]{1,0:T(8,128)S(1)} collective-permute-done((f32[64,16384]{1,0:T(8,128)S(1)}, f32[64,16384]{1,0:T(8,128)S(1)}, u32[]{:S(2)}, u32[]{:S(2)}) %collective-permute-start.1) | collective-permute-done | bytes 4194336 | tf_op jit(solution)/shard_map/ppermute | solution.py:41
  127.6 0.5 add.34
  128.1 0.0 copy-start.2
  128.1 1.9 copy-done.2
  130.1 3.4 fusion.13
  133.5 37.7 %psum.35 = f32[64,64]{0,1:T(8,128)S(1)} all-reduce(f32[64,64]{0,1:T(8,128)S(1)} %fusion.13), channel_id=1, replica_groups=mesh['rows'=8,'snaps'=4] {'rows'}, use_global_device_ids=true, to_apply=%region_0.0 | all-reduce | flops 4096 | bytes 32768 | tf_op jit(solution)/shard_map/psum | solution.py:25
  171.2 0.1 copy.6
  171.3 5.8 %cholesky.44 = f32[64,64]{1,0:T(8,128)S(1)} custom-call(f32[64,64]{1,0:T(8,128)S(1)} %fusion.9), custom_call_target="Cholesky" | custom-call | tf_op jit(solution)/shard_map/jit(cholesky)/cholesky | solution.py:19
  177.1 0.6 compare_reduce_fusion.1
  177.8 0.7 fusion.4
  178.5 4.9 custom-call.6
  183.3 0.3 fusion.2
  183.6 5.5 fusion.14
  189.1 11.6 %fusion.15 = f32[64,256]{1,0:T(8,128)} fusion(f32[64,16384]{1,0:T(8,128)S(1)} %fusion.14, f32[16384,256]{1,0:T(8,128)} %param.5), kind=kOutput, calls=%fused_computation.26 | convolution fusion | flops 3221225472 | bytes 21037056 | tf_op jit(solution)/shard_map/dot_general | solution.py:9
  200.7 0.0 all-reduce.3.cloned.1.call-update
  200.7 0.3 all-reduce.5.cloned.1.call-start
  201.0 65.6 %all-reduce.3.cloned.1.call-done = f32[64,256]{1,0:T(8,128)} async-done(((f32[64,256]{1,0:T(8,128)}), f32[64,256]{1,0:T(8,128)}) %all-reduce.3.cloned.1.call-update) | async-done | bytes 65552 | tf_op jit(solution)/shard_map/psum | solution.py:27
  266.5 18.0 %fusion.16 = f32[64,16384]{1,0:T(8,128)S(1)} fusion(f32[64,256]{1,0:T(8,128)} %all-reduce.3.cloned.1.call-done, f32[16384,256]{1,0:T(8,128)} %param.5), kind=kOutput, calls=%fused_computation.27 | convolution fusion | flops 3221225472 | bytes 21037056 | tf_op jit(solution)/shard_map/dot_general | solution.py:9
  284.5 0.1 collective-permute-start.2
  284.6 7.1 %collective-permute-done.2 = f32[64,16384]{1,0:T(8,128)S(1)} collective-permute-done((f32[64,16384]{1,0:T(8,128)S(1)}, f32[64,16384]{1,0:T(8,128)S(1)}, u32[]{:S(2)}, u32[]{:S(2)}) %collective-permute-start.2) | collective-permute-done | bytes 4194336 | tf_op jit(solution)/shard_map/ppermute | solution.py:41
  291.8 2.5 add.35
  294.2 1.5 collective-permute-start.3
  295.7 91.5 %collective-permute-done.3 = f32[64,16384]{1,0:T(8,128)} collective-permute-done((f32[64,16384]{1,0:T(8,128)}, f32[64,16384]{1,0:T(8,128)}, u32[]{:S(2)}, u32[]{:S(2)}) %collective-permute-start.3) | collective-permute-done | bytes 4194336 | tf_op jit(solution)/shard_map/ppermute | solution.py:41
  387.1 3.9 add.36
  391.0 0.0 copy-start.3
  391.0 1.9 copy-done.3
  392.9 3.4 fusion.17
  396.4 36.1 %psum.37 = f32[64,64]{0,1:T(8,128)S(1)} all-reduce(f32[64,64]{0,1:T(8,128)S(1)} %fusion.17), channel_id=1, replica_groups=mesh['rows'=8,'snaps'=4] {'rows'}, use_global_device_ids=true, to_apply=%region_4.7 | all-reduce | flops 4096 | bytes 32768 | tf_op jit(solution)/shard_map/psum | solution.py:25
  432.5 0.1 copy.8
  432.6 5.8 %cholesky.55 = f32[64,64]{1,0:T(8,128)S(1)} custom-call(f32[64,64]{1,0:T(8,128)S(1)} %fusion.7), custom_call_target="Cholesky" | custom-call | tf_op jit(solution)/shard_map/jit(cholesky)/cholesky | solution.py:19
  438.5 0.6 compare_reduce_fusion
  439.1 0.7 fusion.5
  439.8 4.9 custom-call.7
  444.7 0.3 fusion
  444.9 5.5 fusion.18
  450.4 0.0 copy-start.4
  450.4 1.9 copy-done.4
  452.3 0.0 copy-start.1
  452.3 11.6 %fusion.19 = f32[64,256]{1,0:T(8,128)} fusion(f32[64,16384]{1,0:T(8,128)S(1)} %fusion.18, f32[16384,256]{1,0:T(8,128)} %param.5), kind=kOutput, calls=%fused_computation.30 | convolution fusion | flops 3221225472 | bytes 21037056 | tf_op jit(solution)/shard_map/dot_general | solution.py:9
  463.9 0.0 all-reduce.5.cloned.1.call-update
  464.0 2.3 dynamic-slice_multiply_fusion
  466.3 63.6 %all-reduce.5.cloned.1.call-done = f32[64,256]{1,0:T(8,128)} async-done(((f32[64,256]{1,0:T(8,128)}), f32[64,256]{1,0:T(8,128)}) %all-reduce.5.cloned.1.call-update) | async-done | bytes 65552 | tf_op jit(solution)/shard_map/psum | solution.py:27
  529.8 1.1 fusion.20
  530.9 10.3 %psum.39 = f32[64,64]{1,0:T(8,128)S(1)} all-reduce(f32[64,64]{1,0:T(8,128)S(1)} %fusion.20), channel_id=1, replica_groups=mesh['rows'=8,'snaps'=4] {'snaps'}, use_global_device_ids=true, to_apply=%region_6.9 | all-reduce | flops 4096 | bytes 32768 | tf_op jit(solution)/shard_map/psum | solution.py:46
  541.2 0.6 broadcast_multiply_fusion
  541.8 1.5 copy.13
  543.3 0.0 copy-done.1
  (4 shorter events, 0.1 us)
Async XLA Ops:
  7.2 0.8 copy-start
  7.2 259.4 %all-reduce.3.cloned.1.call-start = ((), (), s32[]{:S(2)}) async-start(), calls=%async_computation | async-start | bytes 131072 | tf_op jit(solution)/shard_map/psum | solution.py:27
  26.0 7.3 %collective-permute-start = (f32[64,16384]{1,0:T(8,128)S(1)}, f32[64,16384]{1,0:T(8,128)S(1)}, u32[]{:S(2)}, u32[]{:S(2)}) collective-permute-start(f32[64,16384]{1,0:T(8,128)S(1)} %fusion.12), channel_id=1, source_target_pairs={{0,1},{1,0},{2,3},{3,2},{4,5},{5,4},{6,7},{7,6},{8,9},{9,8},{10,11... | collective-permute-start | bytes 12582920 | tf_op jit(solution)/shard_map/ppermute | solution.py:41
  33.8 93.8 %collective-permute-start.1 = (f32[64,16384]{1,0:T(8,128)S(1)}, f32[64,16384]{1,0:T(8,128)S(1)}, u32[]{:S(2)}, u32[]{:S(2)}) collective-permute-start(f32[64,16384]{1,0:T(8,128)S(1)} %add.33), channel_id=1, source_target_pairs={{0,2},{1,3},{2,0},{3,1},{4,6},{5,7},{6,4},{7,5},{8,10},{9,11},{10,... | collective-permute-start | bytes 12582920 | tf_op jit(solution)/shard_map/ppermute | solution.py:41
  128.1 1.9 copy-start.2
  200.7 329.1 %all-reduce.5.cloned.1.call-start = ((), (), s32[]{:S(2)}) async-start(), calls=%async_computation.1 | async-start | bytes 131072 | tf_op jit(solution)/shard_map/psum | solution.py:27
  284.5 7.2 %collective-permute-start.2 = (f32[64,16384]{1,0:T(8,128)S(1)}, f32[64,16384]{1,0:T(8,128)S(1)}, u32[]{:S(2)}, u32[]{:S(2)}) collective-permute-start(f32[64,16384]{1,0:T(8,128)S(1)} %fusion.16), channel_id=1, source_target_pairs={{0,1},{1,0},{2,3},{3,2},{4,5},{5,4},{6,7},{7,6},{8,9},{9,8},{10,11... | collective-permute-start | bytes 12582920 | tf_op jit(solution)/shard_map/ppermute | solution.py:41
  294.2 92.9 %collective-permute-start.3 = (f32[64,16384]{1,0:T(8,128)}, f32[64,16384]{1,0:T(8,128)}, u32[]{:S(2)}, u32[]{:S(2)}) collective-permute-start(f32[64,16384]{1,0:T(8,128)} %add.35), channel_id=1, source_target_pairs={{0,2},{1,3},{2,0},{3,1},{4,6},{5,7},{6,4},{7,5},{8,10},{9,11},{10,... | collective-permute-start | bytes 12582920 | tf_op jit(solution)/shard_map/ppermute | solution.py:41
  391.0 1.9 copy-start.3
  450.4 1.9 copy-start.4
  452.3 91.0 %copy-start.1 = (f32[64,256]{1,0:T(8,128)S(1)}, f32[64,256]{1,0:T(8,128)}, u32[]{:S(2)}) copy-start(f32[64,256]{1,0:T(8,128)} %param.6) | copy-start | bytes 196612
Sparse Core Ops, SparseCore 0:
  200.8 65.6 all-reduce.2
  464.1 65.6 all-reduce.4
